TPU v7x, 32 devices: a whole 2x2x4 slice. The times are simulated.
32 devices in a mesh: section: 4 (over x, core), expert: 2 (over y), dp: 4 (over z).
Axes of the slice: x: 2, y: 2, z: 4, core: 2. Of those that a mesh axis runs over, the one named last changes fastest.
Arguments:
- in_flight: bfloat16 [4, 2, 128, 3584], P('section', None, 'expert', 'dp'), may hold values from -6 to 6
- incoming: bfloat16 [2, 128, 3584], P(None, 'expert', 'dp'), may hold values from -6 to 6
- up_proj: bfloat16 [4, 32, 3584, 1152], P('section', 'expert', 'dp'), may hold values from -0.09375 to 0.09375
- down_proj: bfloat16 [4, 32, 1152, 3584], P('section', 'expert', None, 'dp'), may hold values from -0.1875 to 0.1875
- expert_ids: int32 [2, 4, 2, 128, 4], P(None, 'section', None, 'expert'), may hold values from 0 to 31, all different within a row; in each aligned block of 64 rows (0 to 63, 64 to 127, ..., all dimensions but the last counted through in order) at most 12 rows name the same one
- gate_logits: float32 [2, 4, 2, 128, 4], P(None, 'section', None, 'expert'), may hold values from -6 to 6
Outputs:
- states: bfloat16 [2, 4, 2, 128, 3584], P(None, 'section', None, 'expert', 'dp')
Inputs may be any that keep to these rules, and one draw needn't show every extreme that they name: `expert_ids`: each row names 4 different experts. In every aligned block of 64 rows, no expert is named by more than 12 rows, a bound that some block reaches.
All inputs are finite; a program needn't handle non-finite values.
Results may differ from a plain program's by a relative error of at most 0.015.
Values may be sent and summed in bfloat16 or wider, within the bound.
A program may use at most 192 MiB of HBM per device.

v0:
```python
import jax
import jax.numpy as jnp
from jax import lax
from jax.sharding import PartitionSpec as P

MB = 2
TICKS = 2
TOP = 4


def shifted(block, axis, distance):
    devices = range(lax.axis_size(axis))
    route = [(i - distance, i) for i in devices if i - distance in devices]
    return lax.ppermute(block, axis, route)


def gate_weights(logits):
    squashed = jax.nn.sigmoid(logits)
    return 2.5 * squashed / jnp.sum(squashed, axis=-1, keepdims=True)


def routing_slots(routing, experts, capacity):
    pair_ids = routing.reshape(-1)
    onehot = (pair_ids[:, None] == jnp.arange(experts, dtype=jnp.int32)[None, :]).astype(jnp.int32)
    before = jnp.cumsum(onehot, axis=0) - onehot
    slot_numbers = jnp.sum(before * onehot, axis=1)
    return pair_ids * capacity + slot_numbers


def experts_layer(tokens_in, routing, logits, up_weight, down_weight, capacity):
    batch_count, row_count, feature_width = tokens_in.shape
    per_device = up_weight.shape[0]
    groups = lax.axis_size("expert")
    experts = per_device * groups
    slots_total = experts * capacity
    slot_block = per_device * capacity
    flats = jnp.stack([routing_slots(routing[0], experts, capacity)])
    row_ids = jnp.broadcast_to(
        jnp.arange(row_count, dtype=jnp.int32)[:, None], (row_count, TOP)
    ).reshape(-1)

    def fill_table(slot_index):
        return jnp.full((slots_total,), -1, jnp.int32).at[slot_index].set(row_ids)

    sources = jax.vmap(fill_table)(flats)
    offset = jnp.arange(batch_count, dtype=jnp.int32)[:, None] * row_count
    source_index = jnp.where(sources >= 0, sources + offset, -1)
    source_index = (
        source_index.reshape(batch_count, groups, slot_block).transpose(1, 0, 2).reshape(-1)
    )
    flat_tokens = tokens_in.reshape(batch_count * row_count, feature_width)
    outgoing = jnp.where(
        (source_index >= 0)[:, None],
        flat_tokens[jnp.maximum(source_index, 0)],
        jnp.zeros((), flat_tokens.dtype),
    )
    outgoing = outgoing.reshape(groups, batch_count, per_device, capacity, feature_width)
    arrived = lax.all_to_all(outgoing, "expert", split_axis=0, concat_axis=0, tiled=True)
    partial_value = jnp.einsum(
        "gmxcd,xdf->gmxcf", arrived, up_weight, preferred_element_type=jnp.float32
    )
    rounded = lax.optimization_barrier(partial_value.astype(jnp.bfloat16)).astype(jnp.float32)
    summed = lax.psum(rounded.astype(jnp.bfloat16), "dp").astype(jnp.float32)
    hidden = jax.nn.silu(summed).astype(jnp.bfloat16)
    produced = jnp.einsum(
        "gmxcf,xfd->gmxcd", hidden, down_weight, preferred_element_type=jnp.float32
    ).astype(jnp.bfloat16)
    returned = lax.all_to_all(produced, "expert", split_axis=0, concat_axis=0, tiled=True)
    pick_index = (
        flats // slot_block * (batch_count * slot_block)
        + jnp.arange(batch_count, dtype=jnp.int32)[:, None] * slot_block
        + flats % slot_block
    )
    gathered = returned.reshape(-1, feature_width)[pick_index.reshape(-1)].reshape(
        batch_count, row_count, TOP, feature_width
    )
    weights = gate_weights(logits)
    routed_sum = jnp.einsum("mrk,mrkd->mrd", weights, gathered.astype(jnp.float32))
    return (tokens_in.astype(jnp.float32) + routed_sum).astype(jnp.bfloat16)


def body(in_flight, incoming, up_proj, down_proj, expert_ids, gate_logits):
    up_weight = up_proj[0]
    down_weight = down_proj[0]
    groups = lax.axis_size("expert")
    row_count = in_flight.shape[2]
    per_device = up_weight.shape[0]
    capacity = max(2, 3 * row_count * TOP // (2 * per_device * groups))
    current = in_flight[0]
    is_first = lax.axis_index("section") == 0
    states = []
    for tick_index in range(TICKS):
        if tick_index > 0:
            handed_on = shifted(states[-1], "section", 1)
            current = jnp.where(is_first, incoming, handed_on)
        routing = expert_ids[tick_index, 0]
        logits = gate_logits[tick_index, 0]
        pieces = [
            experts_layer(
                current[micro_index : micro_index + 1],
                routing[micro_index : micro_index + 1],
                logits[micro_index : micro_index + 1],
                up_weight,
                down_weight,
                capacity,
            )
            for micro_index in range(MB)
        ]
        result = jnp.concatenate(pieces, axis=0)
        states.append(result)
    return jnp.stack(states)[:, None]


def solution(mesh):
    return jax.shard_map(
        body,
        mesh=mesh,
        in_specs=(
            P("section", None, "expert", "dp"),
            P(None, "expert", "dp"),
            P("section", "expert", "dp", None),
            P("section", "expert", None, "dp"),
            P(None, "section", None, "expert", None),
            P(None, "section", None, "expert", None),
        ),
        out_specs=P(None, "section", None, "expert", "dp"),
        check_vma=False,
    )
```

profile of v0, /device:TPU:2, one launch (start us, length us, event | category | flops | bytes accessed | tf_op | source)
XLA Modules:
  0.0 417.5 jit_solution(6437509623442721821)
XLA Ops:
  6.5 0.7 fusion.147
  7.6 0.6 reduce-window.26
  8.9 1.4 scatter_custom_fusion
  10.3 1.0 slice_bitcast_fusion.1
  11.3 2.3 gather_fusion
  14.1 1.0 copy.45
  15.1 3.5 all-to-all-start
  20.1 1.4 scatter_custom_fusion.1
  21.5 2.3 gather_fusion.2
  25.0 1.0 copy.54
  27.6 0.9 all-to-all-done
  28.6 3.5 all-to-all-start.2
  32.3 14.3 %fusion.37 = bf16[2,1,16,12,1152]{4,3,0,2,1:T(8,128)(2,1)} fusion(bf16[1,16,896,1152]{3,2,1,0:T(8,128)(2,1)} %param.8, bf16[2,1,16,12,896]{4,2,3,1,0:T(8,128)(2,1)S(1)} %all-to-all-done), kind=kOutput, calls=%fused_computation.43 | convolution fusion | flops 793165824 | bytes 34603008 | tf_op jit(solution)/shard_map/gmxcd,xdf->gmxcf/dot_general | solution.py:59
  46.6 14.3 %fusion.34 = bf16[2,1,16,12,1152]{4,3,0,2,1:T(8,128)(2,1)} fusion(bf16[1,16,896,1152]{3,2,1,0:T(8,128)(2,1)} %param.8, bf16[2,1,16,12,896]{4,2,3,1,0:T(8,128)(2,1)S(1)} %all-to-all-done.2), kind=kOutput, calls=%fused_computation.42 | convolution fusion | flops 793165824 | bytes 34603008 | tf_op jit(solution)/shard_map/gmxcd,xdf->gmxcf/dot_general | solution.py:59
  61.9 96.8 %all-reduce.7.cloned.1.call-done = (bf16[2,1,16,12,1152]{4,3,0,2,1:T(8,128)(2,1)}, bf16[2,1,16,12,1152]{4,3,0,2,1:T(8,128)(2,1)}) async-done(((bf16[2,1,16,12,1152]{4,3,0,2,1:T(8,128)(2,1)}, bf16[2,1,16,12,1152]{4,3,0,2,1:T(8,128)(2,1)}), (bf16[2,1,16,12,1152]{4,3,0,2,1:T(8,128)(2,1)}, bf16[2,1,16,12,1152]{4,3,0,2,1:T(8,128)(2,1)})) %all-reduce.7.cloned.1.call-update) | async-done | bytes 1769488 | tf_op jit(solution)/shard_map/psum | solution.py:63
  158.7 15.8 %fusion.74 = bf16[2,1,16,12,896]{4,3,0,2,1:T(8,128)(2,1)S(1)} fusion(bf16[1,16,1152,896]{3,2,1,0:T(8,128)(2,1)} %param.9, bf16[2,1,16,12,1152]{4,3,0,2,1:T(8,128)(2,1)} %get-tuple-element.11), kind=kOutput, calls=%fused_computation.66 | convolution fusion | flops 795721728 | bytes 34603008 | tf_op jit(solution)/shard_map/gmxcf,xfd->gmxcd/dot_general | solution.py:65
  174.5 1.1 copy.56
  175.6 3.5 all-to-all-start.3
  179.2 12.5 %fusion.77 = bf16[2,1,16,12,896]{4,3,0,2,1:T(8,128)(2,1)S(1)} fusion(bf16[1,16,1152,896]{3,2,1,0:T(8,128)(2,1)} %param.9, bf16[2,1,16,12,1152]{4,3,0,2,1:T(8,128)(2,1)S(1)} %copy-done), kind=kOutput, calls=%fused_computation.67 | convolution fusion | flops 795721728 | bytes 34603008 | tf_op jit(solution)/shard_map/gmxcf,xfd->gmxcd/dot_general | solution.py:65
  191.7 1.1 copy.47
  192.8 3.5 all-to-all-start.1
  196.7 1.6 scatter_custom_fusion.2
  198.8 1.2 gather_fusion.3
  200.1 6.2 %all-to-all-done.1 = bf16[2,1,16,12,896]{4,2,3,1,0:T(8,128)(2,1)S(1)} async-done(((bf16[2,1,16,12,896]{4,2,3,1,0:T(8,128)(2,1)}), bf16[2,1,16,12,896]{4,2,3,1,0:T(8,128)(2,1)S(1)}, u32[]{:S(2)}, u32[]{:S(2)}) %all-to-all-start.1) | async-done | bytes 688160 | tf_op jit(solution)/shard_map/all_to_all | solution.py:68
  206.6 1.2 gather_fusion.1
  208.8 1.9 collective-permute-start
  210.8 1.4 scatter_custom_fusion.3
  212.4 3.8 collective-permute-done
  216.2 2.3 gather_fusion.4
  218.9 1.0 copy.63
  219.9 3.5 all-to-all-start.4
  223.4 2.3 gather_fusion.6
  226.0 1.0 copy.72
  227.0 3.8 all-to-all-done.4
  230.8 3.5 all-to-all-start.6
  234.7 14.3 %fusion.31 = bf16[2,1,16,12,1152]{4,3,0,2,1:T(8,128)(2,1)} fusion(bf16[1,16,896,1152]{3,2,1,0:T(8,128)(2,1)} %param.8, bf16[2,1,16,12,896]{4,2,3,1,0:T(8,128)(2,1)S(1)} %all-to-all-done.4), kind=kOutput, calls=%fused_computation.41 | convolution fusion | flops 793165824 | bytes 34603008 | tf_op jit(solution)/shard_map/gmxcd,xdf->gmxcf/dot_general | solution.py:59
  248.9 14.2 %fusion.28 = bf16[2,1,16,12,1152]{4,3,0,2,1:T(8,128)(2,1)} fusion(bf16[1,16,896,1152]{3,2,1,0:T(8,128)(2,1)} %param.8, bf16[2,1,16,12,896]{4,2,3,1,0:T(8,128)(2,1)S(1)} %all-to-all-done.6), kind=kOutput, calls=%fused_computation.40 | convolution fusion | flops 793165824 | bytes 34603008 | tf_op jit(solution)/shard_map/gmxcd,xdf->gmxcf/dot_general | solution.py:59
  263.3 95.7 %all-reduce.5.cloned.1.call-done = (bf16[2,1,16,12,1152]{4,3,0,2,1:T(8,128)(2,1)}, bf16[2,1,16,12,1152]{4,3,0,2,1:T(8,128)(2,1)}) async-done(((bf16[2,1,16,12,1152]{4,3,0,2,1:T(8,128)(2,1)}, bf16[2,1,16,12,1152]{4,3,0,2,1:T(8,128)(2,1)}), (bf16[2,1,16,12,1152]{4,3,0,2,1:T(8,128)(2,1)}, bf16[2,1,16,12,1152]{4,3,0,2,1:T(8,128)(2,1)})) %all-reduce.5.cloned.1.call-update) | async-done | bytes 1769488 | tf_op jit(solution)/shard_map/psum | solution.py:63
  359.0 15.8 %fusion.68 = bf16[2,1,16,12,896]{4,3,0,2,1:T(8,128)(2,1)S(1)} fusion(bf16[1,16,1152,896]{3,2,1,0:T(8,128)(2,1)} %param.9, bf16[2,1,16,12,1152]{4,3,0,2,1:T(8,128)(2,1)} %get-tuple-element.9), kind=kOutput, calls=%fused_computation.64 | convolution fusion | flops 795721728 | bytes 34603008 | tf_op jit(solution)/shard_map/gmxcf,xfd->gmxcd/dot_general | solution.py:65
  374.8 1.1 copy.74
  375.9 3.5 all-to-all-start.7
  379.5 12.5 %fusion.71 = bf16[2,1,16,12,896]{4,3,0,2,1:T(8,128)(2,1)S(1)} fusion(bf16[1,16,1152,896]{3,2,1,0:T(8,128)(2,1)} %param.9, bf16[2,1,16,12,1152]{4,3,0,2,1:T(8,128)(2,1)S(1)} %copy-done.1), kind=kOutput, calls=%fused_computation.65 | convolution fusion | flops 795721728 | bytes 34603008 | tf_op jit(solution)/shard_map/gmxcf,xfd->gmxcd/dot_general | solution.py:65
  392.0 1.1 copy.65
  393.1 3.8 all-to-all-start.5
  397.6 1.2 gather_fusion.7
  398.9 7.9 %all-to-all-done.5 = bf16[2,1,16,12,896]{4,2,3,1,0:T(8,128)(2,1)S(1)} async-done(((bf16[2,1,16,12,896]{4,2,3,1,0:T(8,128)(2,1)}), bf16[2,1,16,12,896]{4,2,3,1,0:T(8,128)(2,1)S(1)}, u32[]{:S(2)}, u32[]{:S(2)}) %all-to-all-start.5) | async-done | bytes 688160 | tf_op jit(solution)/shard_map/all_to_all | solution.py:68
  407.1 1.2 gather_fusion.5
  409.4 0.8 maximum_bitcast_fusion
  (142 shorter events, 12.5 us)
Async XLA Ops:
  15.1 13.5 %all-to-all-start = ((bf16[2,1,16,12,896]{4,2,3,1,0:T(8,128)(2,1)}), bf16[2,1,16,12,896]{4,2,3,1,0:T(8,128)(2,1)S(1)}, u32[]{:S(2)}, u32[]{:S(2)}) async-start(bf16[2,1,16,12,896]{4,2,3,1,0:T(8,128)(2,1)} %copy.45), calls=%async_computation | async-start | bytes 1376256 | tf_op jit(solution)/shard_map/all_to_all | solution.py:58
  26.8 19.8 %copy-start.5 = (s32[32,3]{0,1:T(4,128)}, s32[32,3]{0,1:T(4,128)S(1)}, u32[]{:S(2)}) copy-start(s32[32,3]{0,1:T(4,128)S(1)} %reduce-window.35) | copy-start | bytes 1156
  28.6 18.0 %all-to-all-start.2 = ((bf16[2,1,16,12,896]{4,2,3,1,0:T(8,128)(2,1)}), bf16[2,1,16,12,896]{4,2,3,1,0:T(8,128)(2,1)S(1)}, u32[]{:S(2)}, u32[]{:S(2)}) async-start(bf16[2,1,16,12,896]{4,2,3,1,0:T(8,128)(2,1)} %copy.54), calls=%async_computation.2 | async-start | bytes 1376256 | tf_op jit(solution)/shard_map/all_to_all | solution.py:58
  32.1 126.6 %all-reduce.7.cloned.1.call-start = ((), (), s32[]{:S(2)}) async-start(), calls=%async_computation.9 | async-start | bytes 4718592 | tf_op jit(solution)/shard_map/psum | solution.py:63
  60.9 0.7 slice-start
  60.9 0.8 copy-start.4
  174.5 4.6 %copy-start = (bf16[2,1,16,12,1152]{4,3,0,2,1:T(8,128)(2,1)S(1)}, bf16[2,1,16,12,1152]{4,3,0,2,1:T(8,128)(2,1)}, u32[]{:S(2)}) copy-start(bf16[2,1,16,12,1152]{4,3,0,2,1:T(8,128)(2,1)} %get-tuple-element.12) | copy-start | bytes 2654212
  175.6 17.1 %all-to-all-start.3 = ((bf16[2,1,16,12,896]{4,2,3,1,0:T(8,128)(2,1)}), bf16[2,1,16,12,896]{4,2,3,1,0:T(8,128)(2,1)S(1)}, u32[]{:S(2)}, u32[]{:S(2)}) async-start(bf16[2,1,16,12,896]{4,2,3,1,0:T(8,128)(2,1)} %copy.56), calls=%async_computation.3 | async-start | bytes 1376256 | tf_op jit(solution)/shard_map/all_to_all | solution.py:68
  192.8 13.5 %all-to-all-start.1 = ((bf16[2,1,16,12,896]{4,2,3,1,0:T(8,128)(2,1)}), bf16[2,1,16,12,896]{4,2,3,1,0:T(8,128)(2,1)S(1)}, u32[]{:S(2)}, u32[]{:S(2)}) async-start(bf16[2,1,16,12,896]{4,2,3,1,0:T(8,128)(2,1)} %copy.47), calls=%async_computation.1 | async-start | bytes 1376256 | tf_op jit(solution)/shard_map/all_to_all | solution.py:68
  207.8 1.0 copy-start.2
  207.8 8.4 %copy-start.3 = (bf16[2,64,896]{2,1,0:T(8,128)(2,1)S(1)}, bf16[2,64,896]{2,1,0:T(8,128)(2,1)}, u32[]{:S(2)}) copy-start(bf16[2,64,896]{2,1,0:T(8,128)(2,1)} %param.7) | copy-start | bytes 688132
  208.8 7.3 %collective-permute-start = (bf16[2,64,896]{2,1,0:T(8,128)(2,1)S(1)}, bf16[2,64,896]{2,1,0:T(8,128)(2,1)S(1)}, u32[]{:S(2)}, u32[]{:S(2)}) collective-permute-start(bf16[2,64,896]{2,1,0:T(8,128)(2,1)S(1)} %get-tuple-element.14), channel_id=1, source_target_pairs={{0,8},{8,16},{16,24},{1,9},{9,17},{17,25},{2,10},{10,18},{18,26},{... | collective-permute-start | bytes 688136 | tf_op jit(solution)/shard_map/ppermute | solution.py:14
  219.9 11.0 %all-to-all-start.4 = ((bf16[2,1,16,12,896]{4,2,3,1,0:T(8,128)(2,1)}), bf16[2,1,16,12,896]{4,2,3,1,0:T(8,128)(2,1)S(1)}, u32[]{:S(2)}, u32[]{:S(2)}) async-start(bf16[2,1,16,12,896]{4,2,3,1,0:T(8,128)(2,1)} %copy.63), calls=%async_computation.4 | async-start | bytes 1376256 | tf_op jit(solution)/shard_map/all_to_all | solution.py:58
  230.8 18.1 %all-to-all-start.6 = ((bf16[2,1,16,12,896]{4,2,3,1,0:T(8,128)(2,1)}), bf16[2,1,16,12,896]{4,2,3,1,0:T(8,128)(2,1)S(1)}, u32[]{:S(2)}, u32[]{:S(2)}) async-start(bf16[2,1,16,12,896]{4,2,3,1,0:T(8,128)(2,1)} %copy.72), calls=%async_computation.6 | async-start | bytes 1376256 | tf_op jit(solution)/shard_map/all_to_all | solution.py:58
  234.3 124.7 %all-reduce.5.cloned.1.call-start = ((), (), s32[]{:S(2)}) async-start(), calls=%async_computation.8 | async-start | bytes 4718592 | tf_op jit(solution)/shard_map/psum | solution.py:63
  374.8 4.6 %copy-start.1 = (bf16[2,1,16,12,1152]{4,3,0,2,1:T(8,128)(2,1)S(1)}, bf16[2,1,16,12,1152]{4,3,0,2,1:T(8,128)(2,1)}, u32[]{:S(2)}) copy-start(bf16[2,1,16,12,1152]{4,3,0,2,1:T(8,128)(2,1)} %get-tuple-element.10) | copy-start | bytes 2654212
  375.9 17.1 %all-to-all-start.7 = ((bf16[2,1,16,12,896]{4,2,3,1,0:T(8,128)(2,1)}), bf16[2,1,16,12,896]{4,2,3,1,0:T(8,128)(2,1)S(1)}, u32[]{:S(2)}, u32[]{:S(2)}) async-start(bf16[2,1,16,12,896]{4,2,3,1,0:T(8,128)(2,1)} %copy.74), calls=%async_computation.7 | async-start | bytes 1376256 | tf_op jit(solution)/shard_map/all_to_all | solution.py:68
  393.1 13.8 %all-to-all-start.5 = ((bf16[2,1,16,12,896]{4,2,3,1,0:T(8,128)(2,1)}), bf16[2,1,16,12,896]{4,2,3,1,0:T(8,128)(2,1)S(1)}, u32[]{:S(2)}, u32[]{:S(2)}) async-start(bf16[2,1,16,12,896]{4,2,3,1,0:T(8,128)(2,1)} %copy.65), calls=%async_computation.5 | async-start | bytes 1376256 | tf_op jit(solution)/shard_map/all_to_all | solution.py:68
Sparse Core Ops, SparseCore 0:
  61.0 97.6 all-reduce.6
  263.3 95.6 all-reduce.4
where the time goes:
time: 425 us; the launch traced here: 418 us
  waiting for transfers between devices  215 us (51%)
  matrix products  115 us (27%)
  local copies, waits for them, and re-layouts  35.7 us (8%)
  starting transfers between devices  30.9 us (7%)
  between operations  14.7 us (3%)
  other arithmetic  5.76 us (1%)
    psum x2, waiting for transfers between devices, experts_layer(): summed = lax.psum(rounded.astype(jnp.bfloat16), 'dp').astype(jnp.float32)  193 us
    dot_general x4, matrix products, experts_layer(): jnp.einsum('gmxcd,xdf->gmxcf', arrived, up_weight, preferred_element_type...  57.1 us
    dot_general x4, matrix products, experts_layer(): jnp.einsum('gmxcf,xfd->gmxcd', hidden, down_weight, preferred_element_typ...  56.6 us
    all_to_all x4, starting transfers between devices, experts_layer(): lax.all_to_all(produced, 'expert', split_axis=0, concat_axis=0, tiled=True)  14.4 us
    all_to_all x4, waiting for transfers between devices, experts_layer(): lax.all_to_all(produced, 'expert', split_axis=0, concat_axis=0, tiled=True)  14.1 us
    all_to_all x4, starting transfers between devices, experts_layer(): lax.all_to_all(outgoing, 'expert', split_axis=0, concat_axis=0, tiled=True)  14.1 us
    gather x8, local copies, waits for them, and re-layouts, experts_layer(): flat_tokens[jnp.maximum(source_index, 0)]  9.73 us
  transfers between devices with their start and end apart: 11, of which 7 were waited for; matrix products, arithmetic and copies ran while one was open for 18% of the time, Pallas kernels for 0%

commit v1 on v0

--- a/solution.py
+++ b/solution.py
@@ -1,6 +1,10 @@
+import functools
+
 import jax
 import jax.numpy as jnp
 from jax import lax
+from jax.experimental import pallas as pl
+from jax.experimental.pallas import tpu as pltpu
 from jax.sharding import PartitionSpec as P
 
 MB = 2
@@ -22,7 +26,10 @@
 def routing_slots(routing, experts, capacity):
     pair_ids = routing.reshape(-1)
     onehot = (pair_ids[:, None] == jnp.arange(experts, dtype=jnp.int32)[None, :]).astype(jnp.int32)
-    before = jnp.cumsum(onehot, axis=0) - onehot
+    earlier = jnp.tri(pair_ids.shape[0], k=-1, dtype=jnp.bfloat16)
+    before = jnp.dot(
+        earlier, onehot.astype(jnp.bfloat16), preferred_element_type=jnp.float32
+    ).astype(jnp.int32)
     slot_numbers = jnp.sum(before * onehot, axis=1)
     return pair_ids * capacity + slot_numbers
 
@@ -111,9 +118,371 @@
     return jnp.stack(states)[:, None]
 
 
+MESH = pl.DeviceIdType.MESH
+LAG = 2
+RING = 5
+
+
+def relay_kernel(
+    dims, x_ref, inc_ref, rt_ref, up_hbm, down_hbm, out_ref,
+    x_all, x_disp, route, pick, blend, own, from_left, from_right, to_right, to_left,
+    made, part_out, part_in, up, ring,
+    up_sem, ring_sem, local_sem, tok_send, tok_recv, rt_send, rt_recv, hand_send, hand_recv,
+    right_send, left_send, left_recv, right_recv, part_send, part_recv,
+):
+    sections, chain, rows, per_device, capacity = dims
+    section = lax.axis_index("section")
+    group = lax.axis_index("expert")
+    spot = lax.axis_index("dp")
+    other = 1 - group
+    local = MB * rows
+    slots = 2 * MB * capacity
+    f32, bf16 = jnp.float32, jnp.bfloat16
+    first_section = section == 0
+    has_left, has_right = spot > 0, spot < chain - 1
+    partner = (section, other, spot)
+    my_rows = pl.ds(pl.multiple_of(group * local, local), local)
+
+    def remote(src, dst, send, recv, device):
+        return pltpu.make_async_remote_copy(
+            src_ref=src, dst_ref=dst, send_sem=send, recv_sem=recv,
+            device_id=device, device_id_type=MESH,
+        )
+
+    def load_up(e):
+        return pltpu.make_async_copy(up_hbm.at[e], up.at[e], up_sem.at[e])
+
+    def load_down(e, slot):
+        return pltpu.make_async_copy(down_hbm.at[e], ring.at[slot], ring_sem.at[slot])
+
+    for e in range(per_device):
+        load_up(e).start()
+    for e in range(min(RING, per_device)):
+        load_down(e, e).start()
+    keep_first = pltpu.make_async_copy(x_ref, x_all.at[0, my_rows], local_sem.at[0])
+    keep_first.start()
+    keep_second = pltpu.make_async_copy(inc_ref, x_all.at[1, my_rows], local_sem.at[1])
+
+    @pl.when(first_section)
+    def _():
+        keep_second.start()
+
+    keep_route = pltpu.make_async_copy(rt_ref, route.at[group], local_sem.at[2])
+    keep_route.start()
+
+    barrier = pltpu.get_barrier_semaphore()
+
+    def greet(device):
+        pl.semaphore_signal(barrier, inc=1, device_id=device, device_id_type=MESH)
+
+    greet(partner)
+    for condition, step in ((has_left, -1), (has_right, 1)):
+        @pl.when(condition)
+        def _(step=step):
+            greet((section, group, spot + step))
+    for condition, step in ((section > 0, -1), (section < sections - 1, 1)):
+        @pl.when(condition)
+        def _(step=step):
+            greet((section + step, group, spot))
+            greet((section + step, other, spot))
+    peers = (
+        1 + has_left.astype(jnp.int32) + has_right.astype(jnp.int32)
+        + 2 * (section > 0).astype(jnp.int32) + 2 * (section < sections - 1).astype(jnp.int32)
+    )
+    pl.semaphore_wait(barrier, peers)
+
+    send_route = remote(rt_ref, route.at[group], rt_send, rt_recv, partner)
+    send_route.start()
+    send_first = remote(x_ref, x_all.at[0, my_rows], tok_send.at[0], tok_recv.at[0], partner)
+    send_first.start()
+    send_second = remote(inc_ref, x_all.at[1, my_rows], tok_send.at[1], tok_recv.at[1], partner)
+
+    @pl.when(first_section)
+    def _():
+        send_second.start()
+
+    keep_route.wait()
+    send_route.wait()
+
+    def build_tables(tick):
+        number = lax.broadcasted_iota(jnp.int32, (per_device, local), 0)
+        wanted = (number + group * per_device).astype(f32)
+        half = lax.broadcasted_iota(jnp.int32, (per_device, local), 1) // rows
+        row_a = lax.broadcasted_iota(jnp.int32, (local, local), 0)
+        row_b = lax.broadcasted_iota(jnp.int32, (local, local), 1)
+        earlier = jnp.where(
+            (row_a < row_b) & (row_a // rows == row_b // rows), 1.0, 0.0
+        ).astype(bf16)
+        slot_iota = lax.broadcasted_iota(jnp.int32, (slots, local), 0).astype(f32)
+        for g in range(2):
+            table = route[g, tick]
+            squashed = 1.0 / (1.0 + jnp.exp(-table[TOP:]))
+            gates = 2.5 * squashed / jnp.sum(squashed, axis=0, keepdims=True)
+            named = jnp.zeros((per_device, local), f32)
+            gate_of = jnp.zeros((per_device, local), f32)
+            for k in range(TOP):
+                hit = table[k : k + 1] == wanted
+                named = named + jnp.where(hit, 1.0, 0.0)
+                gate_of = gate_of + jnp.where(hit, gates[k : k + 1], 0.0)
+            rank = jnp.dot(named.astype(bf16), earlier, preferred_element_type=f32)
+            code = jnp.where(
+                named > 0.5, rank + ((g * MB + half) * capacity).astype(f32), -1.0
+            )
+            for e in range(per_device):
+                same = slot_iota == code[e : e + 1]
+                pick[e * slots : (e + 1) * slots, g * local : (g + 1) * local] = jnp.where(
+                    same, 1.0, 0.0
+                ).astype(bf16)
+                blend[g, e * slots : (e + 1) * slots, :] = jnp.where(
+                    same, gate_of[e : e + 1], 0.0
+                ).astype(bf16)
+
+    def group_rows(j):
+        return pl.ds(pl.multiple_of(j * slots, slots), slots)
+
+    for tick in range(TICKS):
+        build_tables(tick)
+        if tick == 0:
+            keep_first.wait()
+            send_first.wait()
+        else:
+            @pl.when(first_section)
+            def _():
+                keep_second.wait()
+                send_second.wait()
+
+            @pl.when(section > 0)
+            def _():
+                for g in range(2):
+                    remote(
+                        x_ref, x_all.at[1, pl.ds(g * local, local)],
+                        hand_send.at[g], hand_recv.at[g], partner,
+                    ).wait_recv()
+        x_disp[...] = jnp.dot(
+            pick[...], x_all[tick], preferred_element_type=f32
+        ).astype(bf16)
+
+        def right_copy(j, tick=tick):
+            return remote(
+                to_right.at[group_rows(j)], from_left.at[tick, group_rows(j)],
+                right_send.at[tick, j], left_recv.at[tick, j], (section, group, spot + 1),
+            )
+
+        def left_copy(j, tick=tick):
+            return remote(
+                to_left.at[group_rows(j)], from_right.at[tick, group_rows(j)],
+                left_send.at[tick, j], right_recv.at[tick, j], (section, group, spot - 1),
+            )
+
+        def step(i, carry, tick=tick):
+            @pl.when(i < per_device)
+            def _():
+                if tick == 0:
+                    pltpu.make_async_copy(up_hbm.at[i], up.at[i], up_sem.at[i]).wait()
+                own[group_rows(i), :] = jnp.dot(
+                    x_disp[group_rows(i), :], up[i], preferred_element_type=f32
+                ).astype(bf16)
+
+            to_r = i - LAG * spot
+
+            @pl.when(has_right & (to_r >= 0) & (to_r < per_device))
+            def _():
+                @pl.when(has_left)
+                def _():
+                    right_copy(to_r).wait_recv()
+                    to_right[group_rows(to_r), :] = (
+                        own[group_rows(to_r), :].astype(f32)
+                        + from_left[tick, group_rows(to_r), :].astype(f32)
+                    ).astype(bf16)
+
+                @pl.when(spot == 0)
+                def _():
+                    to_right[group_rows(to_r), :] = own[group_rows(to_r), :]
+
+                right_copy(to_r).start()
+
+            to_l = i - LAG * (chain - 1 - spot)
+
+            @pl.when(has_left & (to_l >= 0) & (to_l < per_device))
+            def _():
+                @pl.when(has_right)
+                def _():
+                    left_copy(to_l).wait_recv()
+                    to_left[group_rows(to_l), :] = (
+                        own[group_rows(to_l), :].astype(f32)
+                        + from_right[tick, group_rows(to_l), :].astype(f32)
+                    ).astype(bf16)
+
+                @pl.when(spot == chain - 1)
+                def _():
+                    to_left[group_rows(to_l), :] = own[group_rows(to_l), :]
+
+                left_copy(to_l).start()
+
+            last = i - LAG * (chain - 1)
+
+            @pl.when(last >= 0)
+            def _():
+                turn = tick * per_device + last
+                slot = turn % RING
+                block = group_rows(last)
+
+                @pl.when(spot == chain - 1)
+                def _():
+                    right_copy(last).wait_recv()
+                    own[block, :] = (
+                        own[block, :].astype(f32) + from_left[tick, block, :].astype(f32)
+                    ).astype(bf16)
+
+                @pl.when(spot == 0)
+                def _():
+                    left_copy(last).wait_recv()
+                    own[block, :] = (
+                        own[block, :].astype(f32) + from_right[tick, block, :].astype(f32)
+                    ).astype(bf16)
+
+                @pl.when(has_left & has_right)
+                def _():
+                    own[block, :] = (
+                        to_right[block, :].astype(f32) + from_right[tick, block, :].astype(f32)
+                    ).astype(bf16)
+
+                total = own[block, :].astype(f32)
+                hidden = (total / (1.0 + jnp.exp(-total))).astype(bf16)
+                load_down(last, slot).wait()
+                made[block, :] = jnp.dot(
+                    hidden, ring[slot], preferred_element_type=f32
+                ).astype(bf16)
+
+                @pl.when(turn + RING < TICKS * per_device)
+                def _():
+                    load_down((last + RING) % per_device, slot).start()
+
+            return carry
+
+        lax.fori_loop(0, per_device + LAG * (chain - 1), step, 0)
+
+        def combined(g):
+            return lax.dot_general(
+                blend[g], made[...], (((0,), (0,)), ((), ())), preferred_element_type=f32
+            )
+
+        part_out[tick] = combined(other).astype(bf16)
+        send_part = remote(
+            part_out.at[tick], part_in.at[tick], part_send.at[tick], part_recv.at[tick], partner
+        )
+        send_part.start()
+        mine = x_all[tick, my_rows, :].astype(f32) + combined(group)
+        send_part.wait()
+        out_ref[tick] = (mine + part_in[tick].astype(f32)).astype(bf16)
+
+        if tick + 1 < TICKS:
+            @pl.when(section < sections - 1)
+            def _():
+                for g, send in ((group, 0), (other, 1)):
+                    remote(
+                        out_ref.at[tick], x_all.at[1, my_rows], hand_send.at[send],
+                        hand_recv.at[group], (section + 1, g, spot),
+                    ).start()
+
+        def settle(j, carry):
+            @pl.when(has_right)
+            def _():
+                right_copy(j).wait_send()
+
+            @pl.when(has_left)
+            def _():
+                left_copy(j).wait_send()
+
+            return carry
+
+        lax.fori_loop(0, per_device, settle, 0)
+
+    @pl.when(section < sections - 1)
+    def _():
+        for g, send in ((group, 0), (other, 1)):
+            remote(
+                out_ref.at[0], x_all.at[1, my_rows], hand_send.at[send],
+                hand_recv.at[group], (section + 1, g, spot),
+            ).wait_send()
+
+
+def relay_body(sections, chain, in_flight, incoming, up_proj, down_proj, expert_ids, gate_logits):
+    _, _, rows, width = in_flight.shape
+    _, per_device, _, ff = up_proj.shape
+    capacity = max(2, 3 * rows * TOP // (2 * per_device * 2))
+    local = MB * rows
+    slots = 2 * MB * capacity
+    every = per_device * slots
+    bf16, f32 = jnp.bfloat16, jnp.float32
+    routing = jnp.concatenate(
+        [
+            expert_ids[:, 0].astype(f32).reshape(TICKS, local, TOP).transpose(0, 2, 1),
+            gate_logits[:, 0].reshape(TICKS, local, TOP).transpose(0, 2, 1),
+        ],
+        axis=1,
+    )
+    vmem = pl.BlockSpec(memory_space=pltpu.VMEM)
+    anywhere = pl.BlockSpec(memory_space=pl.ANY)
+    dma = pltpu.SemaphoreType.DMA
+    states = pl.pallas_call(
+        functools.partial(relay_kernel, (sections, chain, rows, per_device, capacity)),
+        out_shape=jax.ShapeDtypeStruct((TICKS, local, width), bf16),
+        in_specs=[vmem, vmem, vmem, anywhere, anywhere],
+        out_specs=vmem,
+        scratch_shapes=[
+            pltpu.VMEM((TICKS, 2 * local, width), bf16),
+            pltpu.VMEM((every, width), bf16),
+            pltpu.VMEM((2, TICKS, 2 * TOP, local), f32),
+            pltpu.VMEM((every, 2 * local), bf16),
+            pltpu.VMEM((2, every, local), bf16),
+            pltpu.VMEM((every, ff), bf16),
+            pltpu.VMEM((TICKS, every, ff), bf16),
+            pltpu.VMEM((TICKS, every, ff), bf16),
+            pltpu.VMEM((every, ff), bf16),
+            pltpu.VMEM((every, ff), bf16),
+            pltpu.VMEM((every, width), bf16),
+            pltpu.VMEM((TICKS, local, width), bf16),
+            pltpu.VMEM((TICKS, local, width), bf16),
+            pltpu.VMEM((per_device, width, ff), bf16),
+            pltpu.VMEM((RING, ff, width), bf16),
+            dma((per_device,)),
+            dma((RING,)),
+            dma((3,)),
+            dma((2,)),
+            dma((2,)),
+            dma,
+            dma,
+            dma((2,)),
+            dma((2,)),
+            dma((TICKS, per_device)),
+            dma((TICKS, per_device)),
+            dma((TICKS, per_device)),
+            dma((TICKS, per_device)),
+            dma((TICKS,)),
+            dma((TICKS,)),
+        ],
+        compiler_params=pltpu.CompilerParams(
+            collective_id=0, has_side_effects=True, vmem_limit_bytes=63 * 1024 * 1024
+        ),
+    )(
+        in_flight.reshape(local, width),
+        incoming.reshape(local, width),
+        routing,
+        up_proj[0],
+        down_proj[0],
+    )
+    return states.reshape(TICKS, 1, MB, rows, width)
+
+
 def solution(mesh):
+    shape = dict(mesh.shape)
+    if shape["expert"] == 2:
+        layer = functools.partial(relay_body, shape["section"], shape["dp"])
+    else:
+        layer = body
     return jax.shard_map(
-        body,
+        layer,
         mesh=mesh,
         in_specs=(
             P("section", None, "expert", "dp"),

time: 425 us -> 138 us (0.32); the launches traced: 418 us -> 138 us
  waiting for transfers between devices: 215 us -> 0 us
  Pallas kernels: 0 us -> 134 us
  matrix products: 115 us -> 0 us
  local copies, waits for them, and re-layouts: 35.7 us -> 2.71 us
  starting transfers between devices: 30.9 us -> 0 us
  between operations: 14.7 us -> 0.01 us
  other arithmetic: 5.76 us -> 1.31 us
    psum x2 -> x0, waiting for transfers between devices: 193 us -> none  [experts_layer(): summed = lax.psum(rounded.astype(jnp.bfloat16), 'dp').astype(jnp.float32)]
    pallas_call x0 -> x1, Pallas kernels: none -> 134 us  [relay_body(): pl.pallas_call(functools.partial(relay_kernel, (sections, chain, rows, pe...]
    dot_general x12 -> x0, matrix products: 115 us -> none  [the longest x4 57.1 us: experts_layer(): jnp.einsum('gmxcd,xdf->gmxcf', arrived, up_weight, preferred_element_type...]
    all_to_all x8 -> x0, starting transfers between devices: 28.4 us -> none  [the longest x4 14.4 us: experts_layer(): lax.all_to_all(produced, 'expert', split_axis=0, concat_axis=0, tiled=True)]
    all_to_all x8 -> x0, waiting for transfers between devices: 18.9 us -> none  [the longest x4 14.1 us: experts_layer(): lax.all_to_all(produced, 'expert', split_axis=0, concat_axis=0, tiled=True)]
    gather x12 -> x0, local copies, waits for them, and re-layouts: 14.5 us -> none  [the longest x8 9.73 us: experts_layer(): flat_tokens[jnp.maximum(source_index, 0)]]
    scatter x8 -> x0, local copies, waits for them, and re-layouts: 5.83 us -> none  [fill_table(): return jnp.full((slots_total,), -1, jnp.int32).at[slot_index].set(row_ids)]
  transfers between devices with their start and end apart: 11 -> 0, of which waited for: 7 -> 0; matrix products, arithmetic and copies ran while one was open for 18% -> 0% of each run, Pallas kernels for 0% -> 0%
where the time goes in v1:
time: 138 us
  Pallas kernels  134 us (97%)
  local copies, waits for them, and re-layouts  2.71 us (2%)
    pallas_call x1, Pallas kernels, relay_body(): pl.pallas_call(functools.partial(relay_kernel, (sections, chain, rows, pe...  134 us

profile of v1, /device:TPU:2, one launch (start us, length us, event | category | flops | bytes accessed | tf_op | source)
XLA Modules:
  0.0 138.2 jit_solution(11795094328088696307)
XLA Ops:
  0.0 0.7 convert_element_type.7
  0.7 0.1 convert_element_type.8
  0.8 0.7 copy.8
  1.5 0.1 reshape_squeeze.3
  1.6 0.6 pad_maximum_fusion.rt_ref
  2.2 134.2 %shard_map.64 = bf16[2,128,896]{2,1,0:T(8,128)(2,1)} custom-call(bf16[128,896]{1,0:T(8,128)(2,1)} %bitcast.16, bf16[128,896]{1,0:T(8,128)(2,1)} %bitcast.17, f32[2,8,128]{2,1,0:T(8,128)} %pad_maximum_fusion.rt_ref, bf16[16,896,1152]{2,1,0:T(8,128)(2,1)} %bitcast.13, bf16[16,1152,896]{2,1,0:T(8,128)(2,1)} %bitcast.14), custom_call_target="tpu_custom_call" | custom-call | tf_op jit(solution)/shard_map/pallas_call | solution.py:428
  136.4 1.8 %copy.11 = bf16[2,1,2,64,896]{4,3,2,1,0:T(8,128)(2,1)} copy(bf16[2,1,2,64,896]{4,3,2,1,0:T(8,128)(2,1)} %bitcast.15) | data formatting | bytes 917504
  (1 shorter events, 0.0 us)

commit v2 on v0

--- a/solution.py
+++ b/solution.py
@@ -1,6 +1,10 @@
+import functools
+
 import jax
 import jax.numpy as jnp
 from jax import lax
+from jax.experimental import pallas as pl
+from jax.experimental.pallas import tpu as pltpu
 from jax.sharding import PartitionSpec as P
 
 MB = 2
@@ -22,7 +26,10 @@
 def routing_slots(routing, experts, capacity):
     pair_ids = routing.reshape(-1)
     onehot = (pair_ids[:, None] == jnp.arange(experts, dtype=jnp.int32)[None, :]).astype(jnp.int32)
-    before = jnp.cumsum(onehot, axis=0) - onehot
+    earlier = jnp.tri(pair_ids.shape[0], k=-1, dtype=jnp.bfloat16)
+    before = jnp.dot(
+        earlier, onehot.astype(jnp.bfloat16), preferred_element_type=jnp.float32
+    ).astype(jnp.int32)
     slot_numbers = jnp.sum(before * onehot, axis=1)
     return pair_ids * capacity + slot_numbers
 
@@ -111,9 +118,434 @@
     return jnp.stack(states)[:, None]
 
 
+MESH = pl.DeviceIdType.MESH
+LAG = 2
+RING = 5
+UNITS = TICKS * MB
+
+
+def relay_kernel(
+    dims, x_ref, inc_ref, rt_ref, up_hbm, down_hbm, out_ref,
+    x_all, x_disp, route, pick, blend, own, from_left, from_right, to_right, to_left,
+    made, gathered, part_out, part_in, up, ring,
+    up_sem, ring_sem, local_sem, tok_send, tok_recv, rt_send, rt_recv, hand_send, hand_recv,
+    right_send, left_send, left_recv, right_recv, part_send, part_recv,
+):
+    sections, chain, rows, per_device, capacity = dims
+    section = lax.axis_index("section")
+    group = lax.axis_index("expert")
+    spot = lax.axis_index("dp")
+    other = 1 - group
+    slots = 2 * capacity
+    pair_rows = 2 * slots
+    padded = (slots + 15) // 16 * 16
+    pairs = per_device // 2
+    total_groups = UNITS * pairs
+    kept = 2 * pairs
+    f32, bf16 = jnp.float32, jnp.bfloat16
+    has_left, has_right = spot > 0, spot < chain - 1
+    partner = (section, other, spot)
+    my_rows = pl.ds(pl.multiple_of(group * rows, rows), rows)
+    other_rows = pl.ds(pl.multiple_of(other * rows, rows), rows)
+
+    def remote(src, dst, send, recv, device):
+        return pltpu.make_async_remote_copy(
+            src_ref=src, dst_ref=dst, send_sem=send, recv_sem=recv,
+            device_id=device, device_id_type=MESH,
+        )
+
+    def load_up(e):
+        return pltpu.make_async_copy(up_hbm.at[e], up.at[e], up_sem.at[e])
+
+    def load_down(e, slot):
+        return pltpu.make_async_copy(down_hbm.at[e], ring.at[slot], ring_sem.at[slot])
+
+    for e in range(per_device):
+        load_up(e).start()
+    for e in range(min(RING, per_device)):
+        load_down(e, e).start()
+    def source(u):
+        return x_ref.at[u] if u < MB else inc_ref.at[u - MB]
+
+    def keep(u):
+        return pltpu.make_async_copy(source(u), x_all.at[u, my_rows], local_sem.at[u])
+
+    def exchange(u):
+        return remote(
+            source(u), x_all.at[u, my_rows], tok_send.at[u], tok_recv.at[u], partner
+        )
+
+    first_section = section == 0
+    for u in range(UNITS):
+        if u < MB:
+            keep(u).start()
+        else:
+            @pl.when(first_section)
+            def _(u=u):
+                keep(u).start()
+
+    keep_route = pltpu.make_async_copy(rt_ref, route.at[group], local_sem.at[UNITS])
+    keep_route.start()
+
+    barrier = pltpu.get_barrier_semaphore()
+
+    def greet(device):
+        pl.semaphore_signal(barrier, inc=1, device_id=device, device_id_type=MESH)
+
+    greet(partner)
+    for condition, step in ((has_left, -1), (has_right, 1)):
+        @pl.when(condition)
+        def _(step=step):
+            greet((section, group, spot + step))
+    for condition, step in ((section > 0, -1), (section < sections - 1, 1)):
+        @pl.when(condition)
+        def _(step=step):
+            greet((section + step, group, spot))
+            greet((section + step, other, spot))
+    peers = (
+        1 + has_left.astype(jnp.int32) + has_right.astype(jnp.int32)
+        + 2 * (section > 0).astype(jnp.int32) + 2 * (section < sections - 1).astype(jnp.int32)
+    )
+    pl.semaphore_wait(barrier, peers)
+
+    send_route = remote(rt_ref, route.at[group], rt_send, rt_recv, partner)
+    send_route.start()
+    for u in range(UNITS):
+        if u < MB:
+            exchange(u).start()
+        else:
+            @pl.when(first_section)
+            def _(u=u):
+                exchange(u).start()
+
+    keep_route.wait()
+    send_route.wait()
+
+    def build_tables(u):
+        local = 2 * rows
+        number = lax.broadcasted_iota(jnp.int32, (per_device, local), 0)
+        wanted = (number + group * per_device).astype(f32)
+        lane = lax.broadcasted_iota(jnp.int32, (per_device, local), 1)
+        row_a = lax.broadcasted_iota(jnp.int32, (local, local), 0)
+        row_b = lax.broadcasted_iota(jnp.int32, (local, local), 1)
+        earlier = jnp.where(
+            (row_a < row_b) & (row_a // rows == row_b // rows), 1.0, 0.0
+        ).astype(bf16)
+        table_lane = lax.broadcasted_iota(jnp.int32, (2 * TOP, local), 1)
+        table = jnp.where(table_lane < rows, route[0, u], route[1, u])
+        squashed = 1.0 / (1.0 + jnp.exp(-table[TOP:]))
+        gates = 2.5 * squashed / jnp.sum(squashed, axis=0, keepdims=True)
+        named = jnp.zeros((per_device, local), f32)
+        gate_of = jnp.zeros((per_device, local), f32)
+        for k in range(TOP):
+            hit = table[k : k + 1] == wanted
+            named = named + jnp.where(hit, 1.0, 0.0)
+            gate_of = gate_of + jnp.where(hit, gates[k : k + 1], 0.0)
+        rank = jnp.dot(named.astype(bf16), earlier, preferred_element_type=f32)
+        code = jnp.where(
+            named > 0.5, rank + jnp.where(lane < rows, 0.0, float(capacity)), -1000.0
+        )
+        wide = lax.broadcasted_iota(jnp.int32, (2 * padded, local), 0).astype(f32)
+        tight = lax.broadcasted_iota(jnp.int32, (pair_rows, local), 0).astype(f32)
+        for p in range(pairs):
+            one, two = code[2 * p : 2 * p + 1], code[2 * p + 1 : 2 * p + 2]
+            pick[2 * p * padded : 2 * (p + 1) * padded, :] = (
+                jnp.where(wide == one, 1.0, 0.0) + jnp.where(wide - float(padded) == two, 1.0, 0.0)
+            ).astype(bf16)
+            blend[u, p * pair_rows : (p + 1) * pair_rows, :] = (
+                jnp.where(tight == one, gate_of[2 * p : 2 * p + 1], 0.0)
+                + jnp.where(tight - float(slots) == two, gate_of[2 * p + 1 : 2 * p + 2], 0.0)
+            ).astype(bf16)
+
+    def kept_rows(j):
+        return pl.ds(pl.multiple_of((j % kept) * pair_rows, pair_rows), pair_rows)
+
+    def right_copy(j):
+        return remote(
+            to_right.at[kept_rows(j)], from_left.at[j],
+            right_send.at[j], left_recv.at[j], (section, group, spot + 1),
+        )
+
+    def left_copy(j):
+        return remote(
+            to_left.at[kept_rows(j)], from_right.at[j],
+            left_send.at[j], right_recv.at[j], (section, group, spot - 1),
+        )
+
+    def part_copy(u):
+        return remote(part_out.at[u], part_in.at[u], part_send.at[u], part_recv.at[u], partner)
+
+    def hand_copy(m, g, which):
+        return remote(
+            out_ref.at[m], x_all.at[m + MB, my_rows], hand_send.at[m, which],
+            hand_recv.at[m, group], (section + 1, g, spot),
+        )
+
+    deep = LAG * (chain - 1)
+
+    def step(i, carry):
+        for u in range(UNITS):
+            @pl.when(i == u * pairs)
+            def _(u=u):
+                if u < MB:
+                    keep(u).wait()
+                    exchange(u).wait()
+                else:
+                    @pl.when(first_section)
+                    def _():
+                        keep(u).wait()
+                        exchange(u).wait()
+
+                    @pl.when(section > 0)
+                    def _():
+                        for g in range(2):
+                            remote(
+                                x_ref.at[0], x_all.at[u, pl.ds(g * rows, rows)],
+                                hand_send.at[u - MB, g], hand_recv.at[u - MB, g], partner,
+                            ).wait_recv()
+
+        @pl.when((i < total_groups) & (i % pairs == 0))
+        def _():
+            u = i // pairs
+            build_tables(u)
+            x_disp[...] = jnp.dot(
+                pick[...], x_all[u], preferred_element_type=f32
+            ).astype(bf16)
+
+        @pl.when(i < total_groups)
+        def _():
+            pair = i % pairs
+
+            @pl.when(i < pairs)
+            def _():
+                for t in range(2):
+                    e = 2 * pair + t
+                    pltpu.make_async_copy(up_hbm.at[e], up.at[e], up_sem.at[e]).wait()
+
+            halves = []
+            for t in range(2):
+                e = 2 * pair + t
+                block = x_disp[pl.ds(pl.multiple_of(e * padded, padded), padded), :]
+                halves.append(jnp.dot(block, up[e], preferred_element_type=f32)[:slots])
+            own[kept_rows(i), :] = jnp.concatenate(halves, axis=0).astype(bf16)
+
+        to_r = i - LAG * spot
+
+        @pl.when(has_right & (to_r >= 0) & (to_r < total_groups))
+        def _():
+            @pl.when(to_r >= kept)
+            def _():
+                right_copy(to_r - kept).wait_send()
+
+            @pl.when(has_left)
+            def _():
+                right_copy(to_r).wait_recv()
+                to_right[kept_rows(to_r), :] = (
+                    own[kept_rows(to_r), :].astype(f32) + from_left[to_r].astype(f32)
+                ).astype(bf16)
+
+            @pl.when(spot == 0)
+            def _():
+                to_right[kept_rows(to_r), :] = own[kept_rows(to_r), :]
+
+            right_copy(to_r).start()
+
+        to_l = i - LAG * (chain - 1 - spot)
+
+        @pl.when(has_left & (to_l >= 0) & (to_l < total_groups))
+        def _():
+            @pl.when(to_l >= kept)
+            def _():
+                left_copy(to_l - kept).wait_send()
+
+            @pl.when(has_right)
+            def _():
+                left_copy(to_l).wait_recv()
+                to_left[kept_rows(to_l), :] = (
+                    own[kept_rows(to_l), :].astype(f32) + from_right[to_l].astype(f32)
+                ).astype(bf16)
+
+            @pl.when(spot == chain - 1)
+            def _():
+                to_left[kept_rows(to_l), :] = own[kept_rows(to_l), :]
+
+            left_copy(to_l).start()
+
+        last = i - deep
+
+        @pl.when((last >= 0) & (last < total_groups))
+        def _():
+            block = kept_rows(last)
+
+            @pl.when(spot == chain - 1)
+            def _():
+                right_copy(last).wait_recv()
+                own[block, :] = (
+                    own[block, :].astype(f32) + from_left[last].astype(f32)
+                ).astype(bf16)
+
+            @pl.when(spot == 0)
+            def _():
+                left_copy(last).wait_recv()
+                own[block, :] = (
+                    own[block, :].astype(f32) + from_right[last].astype(f32)
+                ).astype(bf16)
+
+            @pl.when(has_left & has_right)
+            def _():
+                own[block, :] = (
+                    to_right[block, :].astype(f32) + from_right[last].astype(f32)
+                ).astype(bf16)
+
+            total = own[block, :].astype(f32)
+            hidden = total / (1.0 + jnp.exp(-total))
+            halves = []
+            for t in range(2):
+                turn = 2 * last + t
+                slot = turn % RING
+                load_down(turn % per_device, slot).wait()
+                halves.append(jnp.dot(
+                    hidden[t * slots : (t + 1) * slots].astype(bf16), ring[slot],
+                    preferred_element_type=f32,
+                ))
+            made[kept_rows(last), :] = jnp.concatenate(halves, axis=0).astype(bf16)
+            for t in range(2):
+                turn = 2 * last + t
+
+                @pl.when(turn + RING < 2 * total_groups)
+                def _(turn=turn):
+                    load_down((turn + RING) % per_device, turn % RING).start()
+
+        @pl.when((last >= pairs) & (last % pairs == 0) & (last <= total_groups))
+        def _():
+            u = last // pairs - 1
+            part_copy(u).wait()
+            result = (
+                x_all[u, my_rows, :].astype(f32)
+                + gathered[my_rows, :]
+                + part_in[u].astype(f32)
+            )
+            out_ref[u] = result.astype(bf16)
+
+            @pl.when((u < UNITS - MB) & (section < sections - 1))
+            def _():
+                hand_copy(u, group, 0).start()
+                hand_copy(u, other, 1).start()
+
+        @pl.when((last >= 0) & (last < total_groups) & (last % pairs == pairs - 1))
+        def _():
+            u = last // pairs
+            span = pairs * pair_rows
+            output = made[pl.ds(pl.multiple_of((u % 2) * span, span), span), :]
+            gathered[...] = lax.dot_general(
+                blend[u], output, (((0,), (0,)), ((), ())), preferred_element_type=f32
+            )
+            part_out[u] = gathered[other_rows, :].astype(bf16)
+            part_copy(u).start()
+
+        return carry
+
+    lax.fori_loop(0, total_groups + deep + 1, step, 0)
+
+    def settle(j, carry):
+        @pl.when(has_right)
+        def _():
+            right_copy(j).wait_send()
+
+        @pl.when(has_left)
+        def _():
+            left_copy(j).wait_send()
+
+        return carry
+
+    lax.fori_loop(total_groups - kept, total_groups, settle, 0)
+
+    @pl.when(section < sections - 1)
+    def _():
+        for m in range(UNITS - MB):
+            hand_copy(m, group, 0).wait_send()
+            hand_copy(m, other, 1).wait_send()
+
+
+def relay_body(sections, chain, in_flight, incoming, up_proj, down_proj, expert_ids, gate_logits):
+    _, _, rows, width = in_flight.shape
+    _, per_device, _, ff = up_proj.shape
+    capacity = max(2, 3 * rows * TOP // (2 * per_device * 2))
+    slots = 2 * capacity
+    padded = (slots + 15) // 16 * 16
+    pairs = per_device // 2
+    every = per_device * slots
+    bf16, f32 = jnp.bfloat16, jnp.float32
+    routing = jnp.concatenate(
+        [
+            expert_ids[:, 0].astype(f32).reshape(UNITS, rows, TOP).transpose(0, 2, 1),
+            gate_logits[:, 0].reshape(UNITS, rows, TOP).transpose(0, 2, 1),
+        ],
+        axis=1,
+    )
+    routing = jnp.concatenate([routing, routing], axis=2)
+    vmem = pl.BlockSpec(memory_space=pltpu.VMEM)
+    anywhere = pl.BlockSpec(memory_space=pl.ANY)
+    dma = pltpu.SemaphoreType.DMA
+    states = pl.pallas_call(
+        functools.partial(relay_kernel, (sections, chain, rows, per_device, capacity)),
+        out_shape=jax.ShapeDtypeStruct((UNITS, rows, width), bf16),
+        in_specs=[vmem, vmem, vmem, anywhere, anywhere],
+        out_specs=vmem,
+        scratch_shapes=[
+            pltpu.VMEM((UNITS, 2 * rows, width), bf16),
+            pltpu.VMEM((per_device * padded, width), bf16),
+            pltpu.VMEM((2, UNITS, 2 * TOP, 2 * rows), f32),
+            pltpu.VMEM((per_device * padded, 2 * rows), bf16),
+            pltpu.VMEM((UNITS, every, 2 * rows), bf16),
+            pltpu.VMEM((2 * every, ff), bf16),
+            pltpu.VMEM((UNITS * pairs, 2 * slots, ff), bf16),
+            pltpu.VMEM((UNITS * pairs, 2 * slots, ff), bf16),
+            pltpu.VMEM((2 * every, ff), bf16),
+            pltpu.VMEM((2 * every, ff), bf16),
+            pltpu.VMEM((2 * every, width), bf16),
+            pltpu.VMEM((2 * rows, width), f32),
+            pltpu.VMEM((UNITS, rows, width), bf16),
+            pltpu.VMEM((UNITS, rows, width), bf16),
+            pltpu.VMEM((per_device, width, ff), bf16),
+            pltpu.VMEM((RING, ff, width), bf16),
+            dma((per_device,)),
+            dma((RING,)),
+            dma((UNITS + 1,)),
+            dma((UNITS,)),
+            dma((UNITS,)),
+            dma,
+            dma,
+            dma((UNITS - MB, 2)),
+            dma((UNITS - MB, 2)),
+            dma((UNITS * pairs,)),
+            dma((UNITS * pairs,)),
+            dma((UNITS * pairs,)),
+            dma((UNITS * pairs,)),
+            dma((UNITS,)),
+            dma((UNITS,)),
+        ],
+        compiler_params=pltpu.CompilerParams(
+            collective_id=0, has_side_effects=True, vmem_limit_bytes=63 * 1024 * 1024
+        ),
+    )(
+        in_flight[0],
+        incoming,
+        routing,
+        up_proj[0],
+        down_proj[0],
+    )
+    return states.reshape(TICKS, 1, MB, rows, width)
+
+
 def solution(mesh):
+    shape = dict(mesh.shape)
+    if shape["expert"] == 2:
+        layer = functools.partial(relay_body, shape["section"], shape["dp"])
+    else:
+        layer = body
     return jax.shard_map(
-        body,
+        layer,
         mesh=mesh,
         in_specs=(
             P("section", None, "expert", "dp"),

time: 425 us -> 120 us (0.28); the launches traced: 418 us -> 120 us
  waiting for transfers between devices: 215 us -> 0 us
  Pallas kernels: 0 us -> 116 us
  matrix products: 115 us -> 0 us
  local copies, waits for them, and re-layouts: 35.7 us -> 1.82 us
  starting transfers between devices: 30.9 us -> 0 us
  between operations: 14.7 us -> 0.01 us
    psum x2 -> x0, waiting for transfers between devices: 193 us -> none  [experts_layer(): summed = lax.psum(rounded.astype(jnp.bfloat16), 'dp').astype(jnp.float32)]
    pallas_call x0 -> x1, Pallas kernels: none -> 116 us  [relay_body(): pl.pallas_call(functools.partial(relay_kernel, (sections, chain, rows, pe...]
    dot_general x12 -> x0, matrix products: 115 us -> none  [the longest x4 57.1 us: experts_layer(): jnp.einsum('gmxcd,xdf->gmxcf', arrived, up_weight, preferred_element_type...]
    all_to_all x8 -> x0, starting transfers between devices: 28.4 us -> none  [the longest x4 14.4 us: experts_layer(): lax.all_to_all(produced, 'expert', split_axis=0, concat_axis=0, tiled=True)]
    all_to_all x8 -> x0, waiting for transfers between devices: 18.9 us -> none  [the longest x4 14.1 us: experts_layer(): lax.all_to_all(produced, 'expert', split_axis=0, concat_axis=0, tiled=True)]
    gather x12 -> x0, local copies, waits for them, and re-layouts: 14.5 us -> none  [the longest x8 9.73 us: experts_layer(): flat_tokens[jnp.maximum(source_index, 0)]]
    scatter x8 -> x0, local copies, waits for them, and re-layouts: 5.83 us -> none  [fill_table(): return jnp.full((slots_total,), -1, jnp.int32).at[slot_index].set(row_ids)]
    convert_element_type x4 -> x0, local copies, waits for them, and re-layouts: 4.32 us -> none  [experts_layer(): produced = jnp.einsum('gmxcf,xfd->gmxcd', hidden, down_weight, preferred_...]
  transfers between devices with their start and end apart: 11 -> 0, of which waited for: 7 -> 0; matrix products, arithmetic and copies ran while one was open for 18% -> 0% of each run, Pallas kernels for 0% -> 0%
where the time goes in v2:
time: 120 us
  Pallas kernels  116 us (97%)
  other arithmetic  2.16 us (2%)
  local copies, waits for them, and re-layouts  1.82 us (2%)
    pallas_call x1, Pallas kernels, relay_body(): pl.pallas_call(functools.partial(relay_kernel, (sections, chain, rows, pe...  116 us

profile of v2, /device:TPU:2, one launch (start us, length us, event | category | flops | bytes accessed | tf_op | source)
XLA Modules:
  0.0 119.7 jit_solution(4673076699483130714)
XLA Ops:
  0.0 0.7 convert_element_type.7
  0.7 1.5 %maximum_maximum_fusion.rt_ref = f32[4,8,128]{2,1,0:T(8,128)} fusion(f32[4,4,64]{2,1,0:T(4,128)} %bitcast.17, f32[4,4,64]{2,1,0:T(4,128)S(1)} %bitcast.16), kind=kLoop, calls=%fused_computation | loop fusion | flops 12288 | bytes 24576 | tf_op jit(solution)/shard_map/concatenate | solution.py:486
  2.2 115.7 %shard_map.64 = bf16[4,64,896]{2,1,0:T(8,128)(2,1)} custom-call(bf16[2,64,896]{2,1,0:T(8,128)(2,1)} %bitcast.15, bf16[2,64,896]{2,1,0:T(8,128)(2,1)} %inc_ref.1, f32[4,8,128]{2,1,0:T(8,128)} %maximum_maximum_fusion.rt_ref, bf16[16,896,1152]{2,1,0:T(8,128)(2,1)} %bitcast.12, bf16[16,1152,896]{2,1,0:T(8,128)(2,1)} %bitcast.13), custom_call_target="tpu_custom_call" | custom-call | tf_op jit(solution)/shard_map/pallas_call | solution.py:490
  117.9 1.8 %copy.9 = bf16[2,1,2,64,896]{4,3,2,1,0:T(8,128)(2,1)} copy(bf16[2,1,2,64,896]{4,3,2,1,0:T(8,128)(2,1)} %bitcast.14) | data formatting | bytes 917504
